TPU v7x, 32 devices: a whole 2x2x4 slice. The times are simulated.
32 devices in a mesh: groups: 2 (over x), wide: 8 (over z, y), tp: 2 (over core).
Axes of the slice: x: 2, y: 2, z: 4, core: 2. Of those that a mesh axis runs over, the one named last changes fastest.
Arguments:
- hidden: bfloat16 [16, 2, 5120], P(('groups', 'wide')), parts along dimension 0, may hold values from -6 to 6
- kv_weight: bfloat16 [5120, 2048], P('tp'), may hold values from -0.078125 to 0.078125
- adapter_down: float32 [2, 2560, 128], P('tp', 'wide'), may hold values from -0.078125 to 0.078125
- adapter_up: float32 [64, 2048], P(None, ('wide', 'tp')), may hold values from -0.375 to 0.375
- key_gain: float32 [128], replicated, may hold values from 0.1 to 1.9
- cache_keys: bfloat16 [16, 4096, 1024], P(('groups', 'wide'), 'tp'), parts along dimension 0, may hold values from -6 to 6
- cache_values: bfloat16 [16, 4096, 1024], P(('groups', 'wide'), 'tp'), parts along dimension 0, may hold values from -6 to 6
- queries: bfloat16 [16, 2, 8192], P(('groups', 'wide')), parts along dimension 0, may hold values from -128 to 128
- lengths: int32 [16], P(('groups', 'wide')), parts along dimension 0, may hold values from 2 to 4094, as said below
- owner_map: int32 [16], P('groups'), parts along dimension 0, may hold values from 0 to 7, each once
Outputs:
- new_entries: bfloat16 [16, 2, 2048], P(('groups', 'wide')), parts along dimension 0
- attended: bfloat16 [16, 2, 8192], P(('groups', 'wide')), parts along dimension 0
There are 2 independent parts, one for each index of `groups`. A program takes and returns all parts, laid end to end along the dimension named above; an argument that names none is the same for every part. Nothing has to cross between parts.
Inputs may be any that keep to these rules, and one draw needn't show every extreme that they name: `lengths`: some row has exactly 4094 cached tokens. `owner_map`: each value appears once.
All inputs are finite; a program needn't handle non-finite values.
Results may differ from a plain program's by a relative error of at most 0.0055.
Values may be sent and summed in bfloat16 or wider, within the bound.
A program may use at most 128 MiB of HBM per device.

v0:
```python
import jax
import jax.numpy as jnp
from jax import lax
from jax.sharding import PartitionSpec as P

Q_HEADS = 64
KV_HEADS = 8
HEAD = 128
RANK = 64
KVD = 1024


ADAPTER_SCALE = 2.0
ROPE_BASE = 1000000.0
NORM_EPSILON = 1e-06
FAR_BELOW = -1e30


def rotate(normed, positions):
    inverse_frequency = ROPE_BASE ** (-(jnp.arange(HEAD // 2, dtype=jnp.float32) * (2.0 / HEAD)))
    angles = positions[:, :, None, None] * inverse_frequency
    cosine = jnp.cos(angles)
    sine_table = jnp.sin(angles)
    lower_half = normed[..., : HEAD // 2]
    upper_half = normed[..., HEAD // 2 :]
    return jnp.concatenate(
        [
            lower_half * cosine - upper_half * sine_table,
            upper_half * cosine + lower_half * sine_table,
        ],
        axis=-1,
    )


def fresh_entries(summed, key_gain, lengths):
    row_count = summed.shape[0]
    key_heads = summed[..., :KVD].reshape(row_count, 2, KV_HEADS, HEAD)
    value_part = summed[..., KVD:]
    normed = (
        key_heads
        * lax.rsqrt(jnp.mean(key_heads * key_heads, axis=-1, keepdims=True) + NORM_EPSILON)
        * key_gain
    )
    positions = (lengths[:, None] + jnp.arange(2, dtype=jnp.int32)[None, :]).astype(jnp.float32)
    new_keys = rotate(normed, positions).reshape(row_count, 2, KVD).astype(jnp.bfloat16)
    return jnp.concatenate([new_keys, value_part.astype(jnp.bfloat16)], axis=-1)


def finish(query_heads, entries, cache_max, cache_total, cache_mix):
    row_count = entries.shape[0]
    new_keys = entries[..., :KVD].reshape(row_count, 2, KV_HEADS, HEAD)
    new_values = entries[..., KVD:].reshape(row_count, 2, KV_HEADS, HEAD)
    scores = jnp.einsum(
        "rsghd,rtgd->rsght", query_heads, new_keys, preferred_element_type=jnp.float32
    ) * HEAD ** (-0.5)
    causal = (jnp.arange(2)[:, None] >= jnp.arange(2)[None, :])[None, :, None, None, :]
    masked = jnp.where(causal, scores, FAR_BELOW)
    row_max = jnp.maximum(cache_max, jnp.max(masked, axis=-1))
    new_weights = jnp.exp(masked - row_max[..., None])
    rescale = jnp.exp(cache_max - row_max)
    mixed = rescale[..., None] * cache_mix + jnp.einsum(
        "rsght,rtgd->rsghd",
        new_weights.astype(jnp.bfloat16),
        new_values,
        preferred_element_type=jnp.float32,
    )
    denominator = rescale * cache_total + jnp.sum(new_weights, axis=-1)
    return (
        (mixed / denominator[..., None]).reshape(row_count, 2, Q_HEADS * HEAD).astype(jnp.bfloat16)
    )


def body(
    hidden,
    kv_weight,
    adapter_down,
    adapter_up,
    key_gain,
    cache_keys,
    cache_values,
    queries,
    lengths,
    owner_map,
):
    row_count = hidden.shape[0]
    local_span = cache_keys.shape[1]
    group = Q_HEADS // KV_HEADS
    tp_index = lax.axis_index("tp")
    wide_index = lax.axis_index("wide")
    shards = lax.axis_size("wide")
    block_rows = adapter_down.shape[1]
    half_rows = kv_weight.shape[0]
    kv_width = kv_weight.shape[1]
    query_heads = queries.reshape(row_count, 2, KV_HEADS, group, HEAD)
    key_block = cache_keys.reshape(row_count, local_span, KV_HEADS, HEAD)
    value_block = cache_values.reshape(row_count, local_span, KV_HEADS, HEAD)
    scores = jnp.einsum(
        "rsghd,rpgd->rsghp", query_heads, key_block, preferred_element_type=jnp.float32
    ) * HEAD ** (-0.5)
    positions = tp_index * local_span + jnp.arange(local_span, dtype=jnp.int32)
    valid = (positions[None, :] < lengths[:, None]).reshape(row_count, 1, 1, 1, local_span)
    masked = jnp.where(valid, scores, FAR_BELOW)
    local_max = jnp.max(masked, axis=-1)
    cache_max = lax.pmax(local_max, "tp")
    weights = jnp.exp(masked - cache_max[..., None])
    local_total = jnp.sum(weights, axis=-1)
    local_mix = jnp.einsum(
        "rsghp,rpgd->rsghd",
        weights.astype(jnp.bfloat16),
        value_block,
        preferred_element_type=jnp.float32,
    )
    up_full = lax.all_gather(adapter_up, ("wide", "tp"), axis=1, tiled=True)
    shard_ids = jnp.arange(shards, dtype=jnp.int32)
    is_owner = owner_map[:, None] == shard_ids[None, :]
    logical_block = jnp.sum(jnp.where(is_owner, shard_ids[:, None], 0), axis=0)
    hidden_half = lax.dynamic_slice_in_dim(hidden, tp_index * half_rows, half_rows, 2)
    hidden_rows = hidden_half.reshape(row_count * 2, half_rows)
    own_block = logical_block[wide_index]
    base_rows = lax.dynamic_slice_in_dim(kv_weight, own_block * block_rows, block_rows, 0)
    down_rows = adapter_down[0]
    adapter_delta = jnp.concatenate(
        [
            jnp.dot(
                down_rows[:, :RANK],
                up_full[:, :KVD],
                preferred_element_type=jnp.float32,
                precision=lax.Precision.HIGHEST,
            ),
            jnp.dot(
                down_rows[:, RANK:],
                up_full[:, KVD:],
                preferred_element_type=jnp.float32,
                precision=lax.Precision.HIGHEST,
            ),
        ],
        axis=1,
    )
    merged_here = (base_rows.astype(jnp.float32) + ADAPTER_SCALE * adapter_delta).astype(
        jnp.bfloat16
    )
    shard_piece = lax.all_gather(merged_here, "wide", axis=0, tiled=True)
    rows_at = jnp.arange(shard_piece.shape[0], dtype=jnp.int32)
    rows_at = jnp.take(logical_block, rows_at // block_rows) * block_rows + rows_at % block_rows
    partial_value = jnp.dot(
        jnp.take(hidden_rows, rows_at, axis=1), shard_piece, preferred_element_type=jnp.float32
    )
    cache_total, cache_mix = lax.psum((local_total, local_mix), "tp")
    summed = lax.psum(partial_value, "tp")
    entries = fresh_entries(summed.reshape(row_count, 2, kv_width), key_gain, lengths)
    attended = finish(query_heads, entries, cache_max, cache_total, cache_mix)
    return (entries, attended)


def solution(mesh):
    return jax.shard_map(
        body,
        mesh=mesh,
        in_specs=(
            P(("groups", "wide"), None, None),
            P("tp", None),
            P("tp", "wide", None),
            P(None, ("wide", "tp")),
            P(),
            P(("groups", "wide"), "tp", None),
            P(("groups", "wide"), "tp", None),
            P(("groups", "wide"), None, None),
            P(("groups", "wide")),
            P("groups"),
        ),
        out_specs=(P(("groups", "wide"), None, None), P(("groups", "wide"), None, None)),
        check_vma=False,
    )
```

profile of v0, /device:TPU:1, one launch (start us, length us, event | category | flops | bytes accessed | tf_op | source)
XLA Modules:
  0.0 209.5 jit_solution(6716138111625984117)
XLA Ops:
  8.1 24.7 %all_gather.6 = f32[64,2048]{1,0:T(8,128)S(1)} all-gather(f32[64,128]{1,0:T(8,128)} %param.13), channel_id=1, replica_groups=mesh['groups'=2,'wide'=8,'tp'=2] {'wide','tp'}, dimensions={1}, use_global_device_ids=true | all-gather | bytes 557056 | tf_op jit(solution)/shard_map/all_gather | solution.py:113
  32.7 2.1 %fusion.34 = f32[320,1024]{1,0:T(8,128)S(1)} fusion(f32[64,2048]{1,0:T(8,128)S(1)} %all_gather.6, f32[320,128]{1,0:T(8,128)} %bitcast.135), kind=kOutput, calls=%fused_computation.29 | convolution fusion | flops 251658240 | bytes 1736704 | tf_op jit(solution)/shard_map/dot_general | solution.py:130
  34.9 2.1 fusion.36
  37.0 0.7 select_reduce_fusion
  37.7 0.7 fusion.67
  39.1 2.9 %fusion.5 = bf16[320,2048]{1,0:T(8,128)(2,1)} fusion(f32[320,1024]{1,0:T(8,128)S(1)} %fusion.34, f32[320,1024]{1,0:T(8,128)S(1)} %fusion.36, bf16[2560,2048]{1,0:T(8,128)(2,1)} %param.11, s32[]{:T(128)S(6)} %select_n.137), kind=kLoop, calls=%fused_computation.7 | loop fusion | flops 3276800 | bytes 5242884 | tf_op jit(solution)/shard_map/convert_element_type | solution.py:139
  42.0 0.0 all-reduce.3.cloned.1.call-start
  42.1 5.4 %copy.78 = bf16[256,8,8,128]{3,2,1,0:T(8,128)(2,1)} copy(bf16[256,8,8,128]{3,1,2,0:T(8,128)(2,1)} %bitcast.131) | data formatting | bytes 8388608
  48.1 3.9 %fusion.68 = (f32[2,8,8]{2,0,1:T(2,128)S(1)}, f32[1,2,8,8,2048]{4,3,1,2,0:T(8,128)S(1)}) fusion(bf16[2048,8,128,1]{2,1,0,3:T(8,128)(2,1)} %bitcast.133, pred[2048]{0:T(1024)(128)(4,1)S(1)} %add_compare_fusion, bf16[1,2,64,128]{3,1,2,0:T(2,128)(2,1)S(1)} %bitcast.142), kind=kOutput, calls=%fused_computation.112 | convolution fusion | flops 67895168 | bytes 5278208 | tf_op jit(solution)/shard_map/rsghd,rpgd->rsghp/dot_general | solution.py:97
  52.1 2.5 %pmax.7 = f32[1,2,8,8]{3,2,1,0:T(8,128)S(1)} all-reduce(f32[1,2,8,8]{3,2,1,0:T(8,128)S(1)} %bitcast.139), channel_id=1, replica_groups=mesh['groups'=2,'wide'=8,'tp'=2] {'tp'}, use_global_device_ids=true, to_apply=%region_4.5 | all-reduce | flops 128 | bytes 1024 | tf_op jit(solution)/shard_map/pmax | solution.py:104
  54.6 3.3 %copy.80 = bf16[256,8,8,128]{3,2,1,0:T(8,128)(2,1)S(1)} copy(bf16[256,8,8,128]{3,1,2,0:T(8,128)(2,1)} %bitcast.132) | data formatting | bytes 8388608
  57.9 1.9 fusion.18
  59.8 0.1 compare_reduce_fusion
  59.9 0.3 fusion.26
  60.2 0.4 copy.52
  60.6 4.5 %fusion.51 = s32[2560]{0:T(1024)S(1)} fusion(s32[]{:T(128)} %bitcast.1, s32[]{:T(128)} %bitcast.2, s32[]{:T(128)} %bitcast.3, s32[]{:T(128)} %bitcast.4, s32[]{:T(128)} %bitcast.5, s32[]{:T(128)} %bitcast.7, s32[]{:T(128)} %bitcast.6), kind=kLoop, calls=%fused_computation.71 | loop fusion | flops 58880 | bytes 10268 | tf_op jit(solution)/shard_map/jit(_take)/gather | solution.py:144
  65.1 0.7 compare_and_fusion
  65.8 0.1 fusion.52
  65.9 5.1 %gather_fusion = bf16[2560,2]{1,0:T(8,128)(2,1)S(1)} fusion(bf16[2,2560]{0,1:T(8,128)(2,1)S(1)} %bitcast.134, s32[3072]{0:T(1024)S(1)} %pad_clamp_fusion), kind=kCustom, calls=%fused_computation | custom fusion | bytes 30720 | tf_op jit(solution)/shard_map/jit(_take)/gather | solution.py:146
  71.0 0.1 multiply_cosine_fusion
  71.1 118.3 %all-gather.2.cloned.1.call-done = bf16[2560,2048]{1,0:T(8,128)(2,1)} async-done(((bf16[320,2048]{1,0:T(8,128)(2,1)}), bf16[2560,2048]{1,0:T(8,128)(2,1)}) %all-gather.2.cloned.1.call-update) | async-done | bytes 10485776 | tf_op jit(solution)/shard_map/all_gather | solution.py:142
  189.4 5.1 %convolution_bitcast_fusion = f32[1,2,2048]{2,1,0:T(2,128)S(1)} fusion(bf16[2560,2048]{1,0:T(8,128)(2,1)} %all-gather.2.cloned.1.call-done, bf16[2560,2]{1,0:T(8,128)(2,1)S(1)} %gather_fusion, pred[2560]{0:T(1024)(128)(4,1)S(1)} %get-tuple-element.4), kind=kOutput, calls=%fused_computation.12 | convolution fusion | flops 20976640 | bytes 10514944 | tf_op jit(solution)/shard_map/dot_general | solution.py:145
  194.5 4.3 %all-reduce = (f32[1,2,2048]{2,1,0:T(2,128)S(1)}, f32[1,2,8,8]{3,2,1,0:T(8,128)S(1)}) all-reduce(f32[1,2,2048]{2,1,0:T(2,128)S(1)} %convolution_bitcast_fusion, f32[1,2,8,8]{3,2,1,0:T(8,128)S(1)} %bitcast.138), channel_id=1, replica_groups=mesh['groups'=2,'wide'=8,'tp'=2] {'tp'}, use_global_device_ids=true, to_apply=%region_1.2 | all-reduce | flops 4224 | bytes 33792 | tf_op jit(solution)/shard_map/psum | solution.py:149
  198.9 0.1 fusion.57
  199.0 0.1 copy.53
  199.0 0.1 multiply_multiply_fusion
  199.1 0.1 subtract_convert_fusion
  199.2 0.3 fusion.69
  199.7 0.1 maximum_bitcast_fusion
  199.7 1.0 fusion.23
  200.8 0.6 convert_element_type.57
  201.4 0.6 pad_maximum_fusion
  (29 shorter events, 0.3 us)
Async XLA Ops:
  8.0 52.2 %copy-start = (bf16[1,2,5120]{2,1,0:T(2,128)(2,1)S(1)}, bf16[1,2,5120]{2,1,0:T(2,128)(2,1)}, u32[]{:S(2)}) copy-start(bf16[1,2,5120]{2,1,0:T(2,128)(2,1)} %param.10) | copy-start | bytes 61444
  8.0 181.4 %all-gather.2.cloned.1.call-start = ((), (), s32[]{:S(2)}) async-start(), calls=%async_computation | async-start | bytes 11796480 | tf_op jit(solution)/shard_map/all_gather | solution.py:142
  42.0 157.7 %all-reduce.3.cloned.1.call-start = ((), (), s32[]{:S(2)}) async-start(), calls=%async_computation.1 | async-start | bytes 131072 | tf_op jit(solution)/shard_map/psum | solution.py:148
  42.1 6.1 %copy-start.2 = (bf16[1,2,8192]{2,1,0:T(2,128)(2,1)S(1)}, bf16[1,2,8192]{2,1,0:T(2,128)(2,1)}, u32[]{:S(2)}) copy-start(bf16[1,2,8192]{2,1,0:T(2,128)(2,1)} %param.17) | copy-start | bytes 98308
  189.4 9.7 %copy-start.1 = (f32[128]{0:T(128)S(1)}, f32[128]{0:T(128)}, u32[]{:S(2)}) copy-start(f32[128]{0:T(128)} %param.14) | copy-start | bytes 1540
Sparse Core Ops, SparseCore 0:
  42.1 147.2 all-gather.1
Sparse Core Ops, SparseCore 1:
  59.9 14.4 all-reduce.2
where the time goes:
time: 210 us; the launch traced here: 209 us
  waiting for transfers between devices  118 us (56%)
  blocking collectives  31.5 us (15%)
  between operations  17.1 us (8%)
  matrix products  16.5 us (8%)
  local copies, waits for them, and re-layouts  15.6 us (7%)
  other arithmetic  10.4 us (5%)
    all_gather x1, waiting for transfers between devices, body(): shard_piece = lax.all_gather(merged_here, 'wide', axis=0, tiled=True)  118 us
    all_gather x1, blocking collectives, body(): up_full = lax.all_gather(adapter_up, ('wide', 'tp'), axis=1, tiled=True)  24.7 us
    unnamed x8, local copies, waits for them, and re-layouts  8.67 us
    dot_general x1, matrix products, body(): jnp.dot(jnp.take(hidden_rows, rows_at, axis=1), shard_piece, preferred_el...  5.12 us
    gather x1, local copies, waits for them, and re-layouts, body(): jnp.take(hidden_rows, rows_at, axis=1)  5.06 us
    gather x2, other arithmetic, body(): jnp.take(logical_block, rows_at // block_rows) * block_rows  4.55 us
    psum x1, blocking collectives, body(): summed = lax.psum(partial_value, 'tp')  4.33 us
  transfers between devices with their start and end apart: 2, of which 1 were waited for; matrix products, arithmetic and copies ran while one was open for 15% of the time, Pallas kernels for 0%

commit v1 on v0

v1 whole, which is shorter than its diff:
```python
import functools

import jax
import jax.numpy as jnp
import numpy as np
from jax import lax
from jax.experimental import pallas as pl
from jax.experimental.pallas import tpu as pltpu
from jax.sharding import PartitionSpec as P

Q_HEADS = 64
KV_HEADS = 8
HEAD = 128
RANK = 64
KVD = 1024

ADAPTER_SCALE = 2.0
ROPE_BASE = 1000000.0
NORM_EPSILON = 1e-06
FAR_BELOW = -1e30
SCORE_SCALE = HEAD ** (-0.5)

LANES = 128
CHUNK = 256
QUERIES = 2 * Q_HEADS
MESH = pl.DeviceIdType.MESH


def window_of(block_rows):
    return -(-block_rows // LANES) * LANES


def kernel(
    n,
    hidden_ref,
    down_ref,
    up_ref,
    gain_ref,
    freq_ref,
    queries_ref,
    lengths_ref,
    owner_ref,
    weight_hbm,
    keys_hbm,
    values_hbm,
    entries_ref,
    attended_ref,
    key_buf,
    value_buf,
    weight_buf,
    scores,
    block_queries,
    query_rows,
    stage_a,
    land_a,
    rows_a,
    rows_b,
    stage_b,
    land_b,
    up_here,
    up_all,
    mine,
    theirs,
    proj_mine,
    proj_theirs,
    key_rows,
    value_rows,
    out_rows,
    key_sem,
    value_sem,
    weight_sem,
    send_a,
    recv_a,
    send_b,
    recv_b,
    send_up,
    recv_up,
    send_x,
    recv_x,
    send_p,
    recv_p,
):
    w = lax.axis_index("wide")
    t = lax.axis_index("tp")
    other = 1 - t
    block_rows = down_ref.shape[1]
    half = weight_hbm.shape[0]
    span = keys_hbm.shape[1]
    key_chunks = span // CHUNK
    weight_chunks = half // CHUNK
    window = window_of(block_rows)

    barrier = pltpu.get_barrier_semaphore()
    for d in range(n):
        peer = lax.rem(w + d, n)
        if d > 0:
            pl.semaphore_signal(
                barrier, inc=1, device_id={"wide": peer, "tp": t}, device_id_type=MESH
            )
        pl.semaphore_signal(
            barrier, inc=1, device_id={"wide": peer, "tp": other}, device_id_type=MESH
        )

    def key_copy(c):
        return pltpu.make_async_copy(
            keys_hbm.at[0, pl.ds(c * CHUNK, CHUNK), :], key_buf.at[c], key_sem.at[c]
        )

    def value_copy(c):
        return pltpu.make_async_copy(
            values_hbm.at[0, pl.ds(c * CHUNK, CHUNK), :], value_buf.at[c], value_sem.at[c]
        )

    def weight_copy(c):
        return pltpu.make_async_copy(
            weight_hbm.at[pl.ds(c * CHUNK, CHUNK), :], weight_buf.at[c], weight_sem.at[c]
        )

    for c in range(key_chunks):
        key_copy(c).start()
    for c in range(key_chunks):
        value_copy(c).start()
    for c in range(weight_chunks):
        weight_copy(c).start()

    owners = [owner_ref[b] for b in range(n)]

    blocks = []
    for b in range(n):
        near = (b * block_rows) // LANES * LANES
        away = b * block_rows - near
        reach = -(-(away + block_rows) // LANES) * LANES
        start = pl.multiple_of(t * half + near, LANES)
        piece = hidden_ref[0, :, pl.ds(start, reach)].astype(jnp.float32)
        piece = piece[:, away : away + block_rows]
        if window > block_rows:
            piece = jnp.concatenate(
                [piece, jnp.zeros((2, window - block_rows), jnp.float32)], axis=1
            )
        blocks.append(piece)
    for d in range(n):
        peer = lax.rem(w + d, n)
        piece = blocks[0]
        for b in range(1, n):
            piece = jnp.where(owners[b] == peer, blocks[b], piece)
        if d == 0:
            land_a[w] = piece
        else:
            stage_a[peer] = piece

    up_here[...] = up_ref[...].astype(jnp.bfloat16)

    pl.semaphore_wait(barrier, 2 * n - 1)

    def a_copy(peer):
        return pltpu.make_async_remote_copy(
            src_ref=stage_a.at[peer],
            dst_ref=land_a.at[w],
            send_sem=send_a.at[peer],
            recv_sem=recv_a.at[w],
            device_id={"wide": peer, "tp": t},
            device_id_type=MESH,
        )

    def a_wait(peer):
        pltpu.make_async_remote_copy(
            src_ref=stage_a.at[peer],
            dst_ref=land_a.at[peer],
            send_sem=send_a.at[peer],
            recv_sem=recv_a.at[peer],
            device_id={"wide": peer, "tp": t},
            device_id_type=MESH,
        ).wait_recv()

    for d in range(1, n):
        a_copy(lax.rem(w + d, n)).start()

    shard = 2 * w + t
    side = lax.div(shard, n)
    slot = lax.rem(shard, n)

    def up_copy(peer):
        return pltpu.make_async_remote_copy(
            src_ref=up_here,
            dst_ref=up_all.at[slot],
            send_sem=send_up.at[peer],
            recv_sem=recv_up.at[slot],
            device_id={"wide": peer, "tp": side},
            device_id_type=MESH,
        )

    for d in range(1, n):
        up_copy(lax.rem(w + d, n)).start()

    @pl.when(side == t)
    def _():
        up_all[slot] = up_here[...]

    @pl.when(side != t)
    def _():
        up_copy(w).start()

    for j in range(Q_HEADS):
        query_rows[2 * j : 2 * j + 2, :] = queries_ref[
            0, :, LANES * j : LANES * (j + 1)
        ].astype(jnp.float32)
    turned = query_rows[...].T
    column_head = lax.shift_right_logical(
        lax.broadcasted_iota(jnp.int32, (HEAD, QUERIES), 1), 4
    )
    for g in range(KV_HEADS):
        block_queries[g * HEAD : (g + 1) * HEAD, :] = jnp.where(
            column_head == g, turned, 0.0
        ).astype(jnp.bfloat16)

    length = lengths_ref[0]
    first = t * span

    def score_step(c, top):
        key_copy(c).wait()
        found = (
            jnp.dot(key_buf[c], block_queries[...], preferred_element_type=jnp.float32)
            * SCORE_SCALE
        )
        position = first + c * CHUNK + lax.broadcasted_iota(jnp.int32, (CHUNK, QUERIES), 0)
        found = jnp.where(position < length, found, FAR_BELOW)
        scores[c] = found
        return jnp.maximum(top, jnp.max(found, axis=0, keepdims=True))

    top = lax.fori_loop(
        0, key_chunks, score_step, jnp.full((1, QUERIES), FAR_BELOW, jnp.float32)
    )

    placed = down_ref[0]
    if window > block_rows:
        placed = jnp.concatenate(
            [placed, jnp.zeros((window - block_rows, 2 * RANK), jnp.float32)], axis=0
        )
    high = placed.astype(jnp.bfloat16)
    low = (placed - high.astype(jnp.float32)).astype(jnp.bfloat16)
    for d in range(1, n):
        a_wait(lax.rem(w + d, n))
    for r in range(n):
        rows_a[2 * r : 2 * r + 2, :] = land_a[r]
    both = jnp.dot(
        rows_a[...].astype(jnp.bfloat16),
        jnp.concatenate([high, low], axis=1),
        preferred_element_type=jnp.float32,
    )
    rows_b[...] = both[:, : 2 * RANK] + both[:, 2 * RANK :]
    for r in range(n):
        stage_b[r] = rows_b[2 * r : 2 * r + 2, :]
    land_b[shard] = stage_b[w]

    def b_copy(peer, side_to):
        return pltpu.make_async_remote_copy(
            src_ref=stage_b.at[peer],
            dst_ref=land_b.at[shard],
            send_sem=send_b.at[2 * peer + side_to],
            recv_sem=recv_b.at[shard],
            device_id={"wide": peer, "tp": side_to},
            device_id_type=MESH,
        )

    def b_wait(peer, side_from):
        pltpu.make_async_remote_copy(
            src_ref=stage_b.at[peer],
            dst_ref=land_b.at[2 * peer + side_from],
            send_sem=send_b.at[2 * peer + side_from],
            recv_sem=recv_b.at[2 * peer + side_from],
            device_id={"wide": peer, "tp": side_from},
            device_id_type=MESH,
        ).wait_recv()

    for d in range(n):
        peer = lax.rem(w + d, n)
        if d > 0:
            b_copy(peer, t).start()
        b_copy(peer, other).start()

    def value_step(c, carry):
        total, mixes = carry
        weights = jnp.exp(scores[c] - top)
        total = total + jnp.sum(weights, axis=0, keepdims=True)
        across = weights.T.astype(jnp.bfloat16)
        value_copy(c).wait()
        added = []
        for p in range(KV_HEADS // 2):
            added.append(
                mixes[p]
                + jnp.dot(
                    across[32 * p : 32 * p + 32, :],
                    value_buf[c, :, 2 * HEAD * p : 2 * HEAD * (p + 1)],
                    preferred_element_type=jnp.float32,
                )
            )
        return total, tuple(added)

    total, mixes = lax.fori_loop(
        0,
        key_chunks,
        value_step,
        (
            jnp.zeros((1, QUERIES), jnp.float32),
            tuple(jnp.zeros((32, 2 * HEAD), jnp.float32) for _ in range(KV_HEADS // 2)),
        ),
    )
    for p in range(KV_HEADS // 2):
        mine[32 * p : 32 * p + 16, :] = mixes[p][:16, :HEAD]
        mine[32 * p + 16 : 32 * p + 32, :] = mixes[p][16:, HEAD:]
    which = lax.broadcasted_iota(jnp.int32, (8, QUERIES), 0)
    mine[QUERIES : QUERIES + 8, :] = jnp.where(which == 0, top, total)
    x_copy = pltpu.make_async_remote_copy(
        src_ref=mine,
        dst_ref=theirs,
        send_sem=send_x,
        recv_sem=recv_x,
        device_id={"wide": w, "tp": other},
        device_id_type=MESH,
    )
    x_copy.start()

    def weight_step(c, carry):
        weight_copy(c).wait()
        start = pl.multiple_of(t * half + c * CHUNK, CHUNK)
        return carry + jnp.dot(
            hidden_ref[0, :, pl.ds(start, CHUNK)],
            weight_buf[c],
            preferred_element_type=jnp.float32,
        )

    proj_mine[...] = lax.fori_loop(
        0, weight_chunks, weight_step, jnp.zeros((2, 2 * KVD), jnp.float32)
    )

    for d in range(n):
        peer = lax.rem(w + d, n)
        if d > 0:
            b_wait(peer, t)
        b_wait(peer, other)
    inner = land_b[0]
    for i in range(1, 2 * n):
        inner = inner + land_b[i]
    inner = jnp.where(t == 0, inner[:, :RANK], inner[:, RANK:]) * ADAPTER_SCALE
    inner_high = inner.astype(jnp.bfloat16)
    inner_low = (inner - inner_high.astype(jnp.float32)).astype(jnp.bfloat16)
    for k in range(n):
        source = t * n + k

        @pl.when(source != shard)
        def _():
            pltpu.make_async_remote_copy(
                src_ref=up_here,
                dst_ref=up_all.at[k],
                send_sem=send_up.at[k],
                recv_sem=recv_up.at[k],
                device_id={"wide": w, "tp": other},
                device_id_type=MESH,
            ).wait_recv()

    up_side = jnp.concatenate([up_all[k] for k in range(n)], axis=1)
    delta = jnp.dot(inner_high, up_side, preferred_element_type=jnp.float32) + jnp.dot(
        inner_low, up_side, preferred_element_type=jnp.float32
    )
    columns = pl.ds(pl.multiple_of(t * KVD, KVD), KVD)
    proj_mine[:, columns] = proj_mine[:, columns] + delta
    p_copy = pltpu.make_async_remote_copy(
        src_ref=proj_mine,
        dst_ref=proj_theirs,
        send_sem=send_p,
        recv_sem=recv_p,
        device_id={"wide": w, "tp": other},
        device_id_type=MESH,
    )
    p_copy.start()

    row_step = lax.broadcasted_iota(jnp.int32, (2 * KV_HEADS, HEAD), 0) & 1
    lane = lax.broadcasted_iota(jnp.int32, (2 * KV_HEADS, HEAD), 1)
    angles = (length + row_step).astype(jnp.float32) * freq_ref[...]
    cosine = jnp.cos(angles)
    sine = jnp.where(lane < HEAD // 2, -jnp.sin(angles), jnp.sin(angles))

    x_copy.wait_recv()
    first_side = t == 0
    lower = jnp.where(first_side, mine[...], theirs[...])
    upper = jnp.where(first_side, theirs[...], mine[...])
    low_top, low_total = lower[QUERIES : QUERIES + 1], lower[QUERIES + 1 : QUERIES + 2]
    up_top, up_total = upper[QUERIES : QUERIES + 1], upper[QUERIES + 1 : QUERIES + 2]
    cache_top = jnp.maximum(low_top, up_top)
    low_factor = jnp.exp(low_top - cache_top)
    up_factor = jnp.exp(up_top - cache_top)
    cache_total = low_factor * low_total + up_factor * up_total

    def as_rows(line):
        return jnp.broadcast_to(line, (QUERIES, QUERIES)).T

    cache_mix = as_rows(low_factor) * lower[:QUERIES] + as_rows(up_factor) * upper[:QUERIES]
    top_rows = as_rows(cache_top)
    total_rows = as_rows(cache_total)

    p_copy.wait_recv()
    summed = proj_mine[...] + proj_theirs[...]
    for g in range(KV_HEADS):
        key_rows[2 * g : 2 * g + 2, :] = summed[:, HEAD * g : HEAD * (g + 1)]
        value_rows[2 * g : 2 * g + 2, :] = summed[:, KVD + HEAD * g : KVD + HEAD * (g + 1)]
    heads = key_rows[...]
    normed = (
        heads
        * lax.rsqrt(jnp.mean(heads * heads, axis=-1, keepdims=True) + NORM_EPSILON)
        * gain_ref[...]
    )
    rotated = normed * cosine + pltpu.roll(normed, HEAD // 2, 1) * sine
    new_keys = rotated.astype(jnp.bfloat16)
    new_values = value_rows[...].astype(jnp.bfloat16)
    key_rows[...] = rotated
    for g in range(KV_HEADS):
        entries_ref[0, :, HEAD * g : HEAD * (g + 1)] = key_rows[2 * g : 2 * g + 2, :].astype(
            jnp.bfloat16
        )
    entries_ref[0, :, KVD:] = summed[:, KVD:].astype(jnp.bfloat16)

    fresh = (
        lax.dot_general(
            query_rows[...].astype(jnp.bfloat16),
            new_keys,
            (((1,), (1,)), ((), ())),
            preferred_element_type=jnp.float32,
        )
        * SCORE_SCALE
    )
    row = lax.broadcasted_iota(jnp.int32, (QUERIES, 2 * KV_HEADS), 0)
    column = lax.broadcasted_iota(jnp.int32, (QUERIES, 2 * KV_HEADS), 1)
    seen = (lax.shift_right_logical(row, 4) == lax.shift_right_logical(column, 1)) & (
        (column & 1) <= (row & 1)
    )
    masked = jnp.where(seen, fresh, FAR_BELOW)
    row_max = jnp.maximum(top_rows[:, :1], jnp.max(masked, axis=-1, keepdims=True))
    new_weights = jnp.exp(masked - row_max)
    rescale = jnp.exp(top_rows - row_max)
    mixed = rescale * cache_mix + jnp.dot(
        new_weights.astype(jnp.bfloat16), new_values, preferred_element_type=jnp.float32
    )
    denominator = rescale * total_rows + jnp.sum(new_weights, axis=-1, keepdims=True)
    out_rows[...] = mixed / denominator
    for j in range(Q_HEADS):
        attended_ref[0, :, LANES * j : LANES * (j + 1)] = out_rows[
            2 * j : 2 * j + 2, :
        ].astype(jnp.bfloat16)

    for d in range(n):
        peer = lax.rem(w + d, n)
        if d > 0:
            a_copy(peer).wait_send()
            up_copy(peer).wait_send()
            b_copy(peer, t).wait_send()
        b_copy(peer, other).wait_send()

    @pl.when(side != t)
    def _():
        up_copy(w).wait_send()

    x_copy.wait_send()
    p_copy.wait_send()


def body(
    hidden,
    kv_weight,
    adapter_down,
    adapter_up,
    key_gain,
    cache_keys,
    cache_values,
    queries,
    lengths,
    owner_map,
):
    n = lax.axis_size("wide")
    half, width = kv_weight.shape
    span = cache_keys.shape[1]
    block_rows = adapter_down.shape[1]
    key_chunks = span // CHUNK
    weight_chunks = half // CHUNK
    window = window_of(block_rows)
    up_columns = adapter_up.shape[1]
    frequency = ROPE_BASE ** (-(np.arange(HEAD // 2, dtype=np.float64) * (2.0 / HEAD)))
    frequency = np.concatenate([frequency, frequency]).astype(np.float32)[None, :]
    f32, bf16 = jnp.float32, jnp.bfloat16
    vmem = pl.BlockSpec(memory_space=pltpu.VMEM)
    smem = pl.BlockSpec(memory_space=pltpu.SMEM)
    hbm = pl.BlockSpec(memory_space=pl.ANY)
    dma = pltpu.SemaphoreType.DMA
    return pl.pallas_call(
        functools.partial(kernel, n),
        out_shape=(
            jax.ShapeDtypeStruct((1, 2, width), bf16),
            jax.ShapeDtypeStruct((1, 2, Q_HEADS * HEAD), bf16),
        ),
        in_specs=[vmem] * 6 + [smem] * 2 + [hbm] * 3,
        out_specs=(vmem, vmem),
        scratch_shapes=[
            pltpu.VMEM((key_chunks, CHUNK, KVD), bf16),
            pltpu.VMEM((key_chunks, CHUNK, KVD), bf16),
            pltpu.VMEM((weight_chunks, CHUNK, width), bf16),
            pltpu.VMEM((key_chunks, CHUNK, QUERIES), f32),
            pltpu.VMEM((KVD, QUERIES), bf16),
            pltpu.VMEM((QUERIES, HEAD), f32),
            pltpu.VMEM((n, 2, window), f32),
            pltpu.VMEM((n, 2, window), f32),
            pltpu.VMEM((2 * n, window), f32),
            pltpu.VMEM((2 * n, 2 * RANK), f32),
            pltpu.VMEM((n, 2, 2 * RANK), f32),
            pltpu.VMEM((2 * n, 2, 2 * RANK), f32),
            pltpu.VMEM((RANK, up_columns), bf16),
            pltpu.VMEM((n, RANK, up_columns), bf16),
            pltpu.VMEM((QUERIES + 8, HEAD), f32),
            pltpu.VMEM((QUERIES + 8, HEAD), f32),
            pltpu.VMEM((2, width), f32),
            pltpu.VMEM((2, width), f32),
            pltpu.VMEM((2 * KV_HEADS, HEAD), f32),
            pltpu.VMEM((2 * KV_HEADS, HEAD), f32),
            pltpu.VMEM((QUERIES, HEAD), f32),
            dma((key_chunks,)),
            dma((key_chunks,)),
            dma((weight_chunks,)),
            dma((n,)),
            dma((n,)),
            dma((2 * n,)),
            dma((2 * n,)),
            dma((n,)),
            dma((n,)),
            dma,
            dma,
            dma,
            dma,
        ],
        compiler_params=pltpu.CompilerParams(
            collective_id=0, has_side_effects=True, vmem_limit_bytes=48 * 1024 * 1024
        ),
    )(
        hidden,
        adapter_down,
        adapter_up,
        key_gain.reshape(1, HEAD),
        jnp.asarray(frequency),
        queries,
        lengths,
        owner_map,
        kv_weight,
        cache_keys,
        cache_values,
    )


def solution(mesh):
    return jax.shard_map(
        body,
        mesh=mesh,
        in_specs=(
            P(("groups", "wide"), None, None),
            P("tp", None),
            P("tp", "wide", None),
            P(None, ("wide", "tp")),
            P(),
            P(("groups", "wide"), "tp", None),
            P(("groups", "wide"), "tp", None),
            P(("groups", "wide"), None, None),
            P(("groups", "wide")),
            P("groups"),
        ),
        out_specs=(P(("groups", "wide"), None, None), P(("groups", "wide"), None, None)),
        check_vma=False,
    )
```

time: 210 us -> 27.7 us (0.13)
  waiting for transfers between devices: 118 us -> 0 us
  blocking collectives: 31.5 us -> 0 us
  Pallas kernels: 0 us -> 17.4 us
  matrix products: 16.5 us -> 0 us
  between operations: 17.1 us -> 1.3 us
  other arithmetic: 10.4 us -> 0 us
  local copies, waits for them, and re-layouts: 15.6 us -> 8.52 us
    all_gather x1 -> x0, waiting for transfers between devices: 118 us -> none  [body(): shard_piece = lax.all_gather(merged_here, 'wide', axis=0, tiled=True)]
    all_gather x1 -> x0, blocking collectives: 24.7 us -> none  [body(): up_full = lax.all_gather(adapter_up, ('wide', 'tp'), axis=1, tiled=True)]
    pallas_call x0 -> x1, Pallas kernels: none -> 17.4 us  [body(): pl.pallas_call(functools.partial(kernel, n), out_shape=(jax.ShapeDtypeStr...]
    dot_general x7 -> x0, matrix products: 16.5 us -> none  [the longest x1 5.12 us: body(): jnp.dot(jnp.take(hidden_rows, rows_at, axis=1), shard_piece, preferred_el...]
    gather x2 -> x0, local copies, waits for them, and re-layouts: 5.76 us -> none  [the longest x1 5.06 us: body(): jnp.take(hidden_rows, rows_at, axis=1)]
    gather x3 -> x0, other arithmetic: 4.56 us -> none  [the longest x2 4.55 us: body(): jnp.take(logical_block, rows_at // block_rows) * block_rows]
    psum x1 -> x0, blocking collectives: 4.33 us -> none  [body(): summed = lax.psum(partial_value, 'tp')]
    convert_element_type x3 -> x0, other arithmetic: 2.94 us -> none  [the longest x1 2.85 us: body(): (base_rows.astype(jnp.float32) + ADAPTER_SCALE * adapter_delta).astype(jn...]
  transfers between devices with their start and end apart: 2 -> 0, of which waited for: 1 -> 0; matrix products, arithmetic and copies ran while one was open for 15% -> 0% of each run, Pallas kernels for 0% -> 0%
where the time goes in v1:
time: 27.7 us; the launch traced here: 27.3 us
  Pallas kernels  17.4 us (63%)
  local copies, waits for them, and re-layouts  8.52 us (31%)
  between operations  1.3 us (5%)
    pallas_call x1, Pallas kernels, body(): pl.pallas_call(functools.partial(kernel, n), out_shape=(jax.ShapeDtypeStr...  17.4 us
    unnamed x18, local copies, waits for them, and re-layouts  8.52 us

profile of v1, /device:TPU:1, one launch (start us, length us, event | category | flops | bytes accessed | tf_op | source)
XLA Modules:
  0.0 27.3 jit_solution(16833615415336491759)
XLA Ops:
  1.3 0.0 copy-start
  1.3 2.2 %copy-done = bf16[1,2048,1024]{2,1,0:T(8,128)(2,1)S(1)} copy-done((bf16[1,2048,1024]{2,1,0:T(8,128)(2,1)S(1)}, bf16[1,2048,1024]{2,1,0:T(8,128)(2,1)}, u32[]{:S(2)}) %copy-start) | copy-done | bytes 4194328
  3.5 0.0 copy-start.1
  3.5 0.9 %copy-done.1 = f32[1,320,128]{2,1,0:T(8,128)S(1)} copy-done((f32[1,320,128]{2,1,0:T(8,128)S(1)}, f32[1,320,128]{2,1,0:T(8,128)}, u32[]{:S(2)}) %copy-start.1) | copy-done | bytes 163864
  4.4 0.0 copy-start.2
  4.4 0.8 %copy-done.2 = f32[64,128]{1,0:T(8,128)S(1)} copy-done((f32[64,128]{1,0:T(8,128)S(1)}, f32[64,128]{1,0:T(8,128)}, u32[]{:S(2)}) %copy-start.2) | copy-done | bytes 32792
  5.1 0.0 copy-start.3
  5.1 0.8 %copy-done.3 = bf16[1,2,8192]{2,1,0:T(2,128)(2,1)S(1)} copy-done((bf16[1,2,8192]{2,1,0:T(2,128)(2,1)S(1)}, bf16[1,2,8192]{2,1,0:T(2,128)(2,1)}, u32[]{:S(2)}) %copy-start.3) | copy-done | bytes 32792
  5.9 0.0 copy-start.4
  5.9 0.7 %copy-done.4 = bf16[1,2,5120]{2,1,0:T(2,128)(2,1)S(1)} copy-done((bf16[1,2,5120]{2,1,0:T(2,128)(2,1)S(1)}, bf16[1,2,5120]{2,1,0:T(2,128)(2,1)}, u32[]{:S(2)}) %copy-start.4) | copy-done | bytes 20504
  6.6 0.0 copy-start.5
  6.6 0.7 %copy-done.5 = f32[128]{0:T(128)S(1)} copy-done((f32[128]{0:T(128)S(1)}, f32[128]{0:T(128)}, u32[]{:S(2)}) %copy-start.5) | copy-done | bytes 536
  7.3 0.0 copy-start.6
  7.3 0.7 %copy-done.6 = s32[8]{0:T(128)S(1)} copy-done((s32[8]{0:T(128)S(1)}, s32[8]{0:T(128)}, u32[]{:S(2)}) %copy-start.6) | copy-done | bytes 56
  7.9 0.0 copy-start.7
  7.9 0.7 %copy-done.7 = f32[1,128]{1,0:T(1,128)S(1)} copy-done((f32[1,128]{1,0:T(1,128)S(1)}, f32[1,128]{1,0:T(1,128)}, u32[]{:S(2)}) %copy-start.7) | copy-done | bytes 536
  8.6 17.4 %shard_map.122 = (bf16[1,2,2048]{2,1,0:T(2,128)(2,1)S(1)}, bf16[1,2,8192]{2,1,0:T(2,128)(2,1)S(1)}) custom-call(bf16[1,2,5120]{2,1,0:T(2,128)(2,1)S(1)} %copy-done.4, f32[1,320,128]{2,1,0:T(8,128)S(1)} %copy-done.1, f32[64,128]{1,0:T(8,128)S(1)} %copy-done.2, f32[1,128]{1,0:T(1,128)S(1)} %bitcast.1, f32[1,128]{1,0:T(1,128)S(1)} %copy-done.7, ...), custom_call_target="tpu_custom_call" | custom-call | tf_op jit(solution)/shard_map/pallas_call | solution.py:493
  26.0 0.6 %copy.16 = bf16[1,2,2048]{2,1,0:T(2,128)(2,1)} copy(bf16[1,2,2048]{2,1,0:T(2,128)(2,1)S(1)} %get-tuple-element.4) | data formatting | bytes 16384
  26.6 0.6 %copy.17 = bf16[1,2,8192]{2,1,0:T(2,128)(2,1)} copy(bf16[1,2,8192]{2,1,0:T(2,128)(2,1)S(1)} %get-tuple-element.5) | data formatting | bytes 65536
Async XLA Ops:
  1.3 2.2 %copy-start = (bf16[1,2048,1024]{2,1,0:T(8,128)(2,1)S(1)}, bf16[1,2048,1024]{2,1,0:T(8,128)(2,1)}, u32[]{:S(2)}) copy-start(bf16[1,2048,1024]{2,1,0:T(8,128)(2,1)} %keys_hbm.1) | copy-start | bytes 12582916
  3.5 0.9 %copy-start.1 = (f32[1,320,128]{2,1,0:T(8,128)S(1)}, f32[1,320,128]{2,1,0:T(8,128)}, u32[]{:S(2)}) copy-start(f32[1,320,128]{2,1,0:T(8,128)} %down_ref.1) | copy-start | bytes 491524
  4.4 0.8 %copy-start.2 = (f32[64,128]{1,0:T(8,128)S(1)}, f32[64,128]{1,0:T(8,128)}, u32[]{:S(2)}) copy-start(f32[64,128]{1,0:T(8,128)} %up_ref.1) | copy-start | bytes 98308
  5.1 0.8 %copy-start.3 = (bf16[1,2,8192]{2,1,0:T(2,128)(2,1)S(1)}, bf16[1,2,8192]{2,1,0:T(2,128)(2,1)}, u32[]{:S(2)}) copy-start(bf16[1,2,8192]{2,1,0:T(2,128)(2,1)} %queries_ref.1) | copy-start | bytes 98308
  5.9 0.7 %copy-start.4 = (bf16[1,2,5120]{2,1,0:T(2,128)(2,1)S(1)}, bf16[1,2,5120]{2,1,0:T(2,128)(2,1)}, u32[]{:S(2)}) copy-start(bf16[1,2,5120]{2,1,0:T(2,128)(2,1)} %hidden_ref.1) | copy-start | bytes 61444
  6.6 0.7 %copy-start.5 = (f32[128]{0:T(128)S(1)}, f32[128]{0:T(128)}, u32[]{:S(2)}) copy-start(f32[128]{0:T(128)} %param.15) | copy-start | bytes 1540
  7.3 0.7 %copy-start.6 = (s32[8]{0:T(128)S(1)}, s32[8]{0:T(128)}, u32[]{:S(2)}) copy-start(s32[8]{0:T(128)} %owner_ref.1) | copy-start | bytes 100
  7.9 0.7 %copy-start.7 = (f32[1,128]{1,0:T(1,128)S(1)}, f32[1,128]{1,0:T(1,128)}, u32[]{:S(2)}) copy-start(f32[1,128]{1,0:T(1,128)} %constant.2.clone.freq_ref) | copy-start | bytes 1540

commit v2 on v1

--- a/solution.py
+++ b/solution.py
@@ -32,6 +32,19 @@
 
 def kernel(
     n,
+    hidden_hbm,
+    down_hbm,
+    up_hbm,
+    gain_hbm,
+    freq_hbm,
+    queries_hbm,
+    lengths_hbm,
+    owner_hbm,
+    weight_hbm,
+    keys_hbm,
+    values_hbm,
+    entries_ref,
+    attended_ref,
     hidden_ref,
     down_ref,
     up_ref,
@@ -40,11 +53,7 @@
     queries_ref,
     lengths_ref,
     owner_ref,
-    weight_hbm,
-    keys_hbm,
-    values_hbm,
-    entries_ref,
-    attended_ref,
+    small_sem,
     key_buf,
     value_buf,
     weight_buf,
@@ -83,12 +92,30 @@
     w = lax.axis_index("wide")
     t = lax.axis_index("tp")
     other = 1 - t
-    block_rows = down_ref.shape[1]
+    block_rows = down_hbm.shape[1]
     half = weight_hbm.shape[0]
     span = keys_hbm.shape[1]
     key_chunks = span // CHUNK
     weight_chunks = half // CHUNK
     window = window_of(block_rows)
+
+    small = [
+        pltpu.make_async_copy(source, target, small_sem.at[i])
+        for i, (source, target) in enumerate(
+            (
+                (owner_hbm, owner_ref),
+                (hidden_hbm, hidden_ref),
+                (up_hbm, up_ref),
+                (queries_hbm, queries_ref),
+                (lengths_hbm, lengths_ref),
+                (down_hbm, down_ref),
+                (gain_hbm, gain_ref),
+                (freq_hbm, freq_ref),
+            )
+        )
+    ]
+    for copy in small:
+        copy.start()
 
     barrier = pltpu.get_barrier_semaphore()
     for d in range(n):
@@ -122,6 +149,9 @@
         value_copy(c).start()
     for c in range(weight_chunks):
         weight_copy(c).start()
+
+    for copy in small[:3]:
+        copy.wait()
 
     owners = [owner_ref[b] for b in range(n)]
 
@@ -199,6 +229,9 @@
     @pl.when(side != t)
     def _():
         up_copy(w).start()
+
+    for copy in small[3:]:
+        copy.wait()
 
     for j in range(Q_HEADS):
         query_rows[2 * j : 2 * j + 2, :] = queries_ref[
@@ -487,8 +520,7 @@
     frequency = np.concatenate([frequency, frequency]).astype(np.float32)[None, :]
     f32, bf16 = jnp.float32, jnp.bfloat16
     vmem = pl.BlockSpec(memory_space=pltpu.VMEM)
-    smem = pl.BlockSpec(memory_space=pltpu.SMEM)
-    hbm = pl.BlockSpec(memory_space=pl.ANY)
+    hbm = pl.BlockSpec(memory_space=pltpu.HBM)
     dma = pltpu.SemaphoreType.DMA
     return pl.pallas_call(
         functools.partial(kernel, n),
@@ -496,9 +528,18 @@
             jax.ShapeDtypeStruct((1, 2, width), bf16),
             jax.ShapeDtypeStruct((1, 2, Q_HEADS * HEAD), bf16),
         ),
-        in_specs=[vmem] * 6 + [smem] * 2 + [hbm] * 3,
+        in_specs=[hbm] * 11,
         out_specs=(vmem, vmem),
         scratch_shapes=[
+            pltpu.VMEM(hidden.shape, bf16),
+            pltpu.VMEM(adapter_down.shape, f32),
+            pltpu.VMEM(adapter_up.shape, f32),
+            pltpu.VMEM((1, HEAD), f32),
+            pltpu.VMEM((1, HEAD), f32),
+            pltpu.VMEM(queries.shape, bf16),
+            pltpu.SMEM(lengths.shape, jnp.int32),
+            pltpu.SMEM(owner_map.shape, jnp.int32),
+            dma((8,)),
             pltpu.VMEM((key_chunks, CHUNK, KVD), bf16),
             pltpu.VMEM((key_chunks, CHUNK, KVD), bf16),
             pltpu.VMEM((weight_chunks, CHUNK, width), bf16),
@@ -535,7 +576,7 @@
             dma,
         ],
         compiler_params=pltpu.CompilerParams(
-            collective_id=0, has_side_effects=True, vmem_limit_bytes=48 * 1024 * 1024
+            collective_id=0, has_side_effects=True, vmem_limit_bytes=62 * 1024 * 1024
         ),
     )(
         hidden,

time: 27.7 us -> 21.8 us (0.79)
  local copies, waits for them, and re-layouts: 8.52 us -> 2.7 us
    unnamed x18 -> x2, local copies, waits for them, and re-layouts: 8.52 us -> 2.7 us
where the time goes in v2:
time: 21.8 us; the launch traced here: 21.6 us
  Pallas kernels  17.6 us (81%)
  local copies, waits for them, and re-layouts  2.7 us (12%)
  between operations  1.29 us (6%)
    pallas_call x1, Pallas kernels, body(): pl.pallas_call(functools.partial(kernel, n), out_shape=(jax.ShapeDtypeStr...  17.6 us
    unnamed x2, local copies, waits for them, and re-layouts  2.7 us

profile of v2, /device:TPU:1, one launch (start us, length us, event | category | flops | bytes accessed | tf_op | source)
XLA Modules:
  0.0 21.6 jit_solution(12543462700572562433)
XLA Ops:
  1.3 17.6 %shard_map.122 = (bf16[1,2,2048]{2,1,0:T(2,128)(2,1)}, bf16[1,2,8192]{2,1,0:T(2,128)(2,1)}) custom-call(bf16[1,2,5120]{2,1,0:T(2,128)(2,1)} %hidden_hbm.1, f32[1,320,128]{2,1,0:T(8,128)} %down_hbm.1, f32[64,128]{1,0:T(8,128)} %up_hbm.1, f32[1,128]{1,0:T(1,128)} %bitcast.1, f32[1,128]{1,0:T(1,128)} %constant.2.clone.freq_hbm, ...), custom_call_target="tpu_custom_call" | custom-call | tf_op jit(solution)/shard_map/pallas_call | solution.py:525
  18.9 1.3 %copy.16 = bf16[1,2,2048]{2,1,0:T(2,128)(2,1)} copy(bf16[1,2,2048]{2,1,0:T(2,128)(2,1)} %get-tuple-element.4) | data formatting | bytes 16384
  20.2 1.4 %copy.17 = bf16[1,2,8192]{2,1,0:T(2,128)(2,1)} copy(bf16[1,2,8192]{2,1,0:T(2,128)(2,1)} %get-tuple-element.5) | data formatting | bytes 65536

commit v3 on v2

--- a/solution.py
+++ b/solution.py
@@ -496,6 +496,15 @@
     p_copy.wait_send()
 
 
+def hand_over(entries_in, attended_in, entries_out, attended_out, entries_sem, attended_sem):
+    entries_copy = pltpu.make_async_copy(entries_in, entries_out, entries_sem)
+    attended_copy = pltpu.make_async_copy(attended_in, attended_out, attended_sem)
+    entries_copy.start()
+    attended_copy.start()
+    entries_copy.wait()
+    attended_copy.wait()
+
+
 def body(
     hidden,
     kv_weight,
@@ -522,7 +531,7 @@
     vmem = pl.BlockSpec(memory_space=pltpu.VMEM)
     hbm = pl.BlockSpec(memory_space=pltpu.HBM)
     dma = pltpu.SemaphoreType.DMA
-    return pl.pallas_call(
+    results = pl.pallas_call(
         functools.partial(kernel, n),
         out_shape=(
             jax.ShapeDtypeStruct((1, 2, width), bf16),
@@ -591,6 +600,13 @@
         cache_keys,
         cache_values,
     )
+    return pl.pallas_call(
+        hand_over,
+        out_shape=tuple(jax.ShapeDtypeStruct(r.shape, r.dtype) for r in results),
+        in_specs=[vmem, vmem],
+        out_specs=(hbm, hbm),
+        scratch_shapes=[dma, dma],
+    )(*results)
 
 
 def solution(mesh):

time: 21.8 us -> 20.6 us (0.945)
  local copies, waits for them, and re-layouts: 2.7 us -> 0 us
  Pallas kernels: 17.6 us -> 19 us
    unnamed x2 -> x0, local copies, waits for them, and re-layouts: 2.7 us -> none
    pallas_call x0 -> x1, Pallas kernels: none -> 1.41 us  [body(): pl.pallas_call(hand_over, out_shape=tuple((jax.ShapeDtypeStruct(r.shape,...]
where the time goes in v3:
time: 20.6 us; the launch traced here: 20.3 us
  Pallas kernels  19 us (92%)
  between operations  1.29 us (6%)
    pallas_call x1, Pallas kernels, body(): pl.pallas_call(functools.partial(kernel, n), out_shape=(jax.ShapeDtypeStr...  17.6 us
    pallas_call x1, Pallas kernels, body(): pl.pallas_call(hand_over, out_shape=tuple((jax.ShapeDtypeStruct(r.shape,...  1.41 us

profile of v3, /device:TPU:1, one launch (start us, length us, event | category | flops | bytes accessed | tf_op | source)
XLA Modules:
  0.0 20.3 jit_solution(14345699789349280417)
XLA Ops:
  1.3 17.6 %shard_map.122 = (bf16[1,2,2048]{2,1,0:T(2,128)(2,1)}, bf16[1,2,8192]{2,1,0:T(2,128)(2,1)}) custom-call(bf16[1,2,5120]{2,1,0:T(2,128)(2,1)} %hidden_hbm.1, f32[1,320,128]{2,1,0:T(8,128)} %down_hbm.1, f32[64,128]{1,0:T(8,128)} %up_hbm.1, f32[1,128]{1,0:T(1,128)} %bitcast.1, f32[1,128]{1,0:T(1,128)} %constant.2.clone.freq_hbm, ...), custom_call_target="tpu_custom_call" | custom-call | tf_op jit(solution)/shard_map/pallas_call | solution.py:534
  18.9 1.4 %shard_map.123 = (bf16[1,2,2048]{2,1,0:T(2,128)(2,1)}, bf16[1,2,8192]{2,1,0:T(2,128)(2,1)}) custom-call(bf16[1,2,2048]{2,1,0:T(2,128)(2,1)} %get-tuple-element.4.entries_in, bf16[1,2,8192]{2,1,0:T(2,128)(2,1)} %get-tuple-element.5.attended_in), custom_call_target="tpu_custom_call" | custom-call | tf_op jit(solution)/shard_map/pallas_call | solution.py:603
